TPU v7x, 256 devices: a whole 4x4x8 slice. The times are simulated.
256 devices in a mesh: tm: 8 (over z_hi, y), row: 8 (over z_lo, core), blk: 4 (over x).
Axes of the slice: x: 4, y: 4, z: 8 (z_hi: 2, z_lo: 4; z = z_hi * 4 + z_lo), core: 2. Of those that a mesh axis runs over, the one named last changes fastest.
Arguments:
- right_side: float32 [32, 32, 16, 8, 384], P('tm', None, 'row', 'blk'), may hold values from -16 to 16
- stiffness: bfloat16 [16, 8, 10, 384, 384], P('row', 'blk'), may hold values from -0.039794922 to 0.039794922
- segments: int32 [16, 8, 10], P('row', 'blk'), may hold values from 1 to 4
- connectivity: int32 [16, 8, 10, 2], P('row', 'blk'), may hold values from 0 to 15, as said below
- lumped_mass: float32 [16, 8, 384], P('row', 'blk'), may hold values from 0.25 to 4
- stiff_diag: float32 [16, 8, 384], P('row', 'blk'), may hold values from 1.5 to 16
Outputs:
- correction: float32 [32, 32, 16, 8, 384], P('tm', None, 'row', 'blk')
Inputs may be any that keep to these rules, and one draw needn't show every extreme that they name: `connectivity`: every named block column lies at most 2 lattice sites from its block row along each lattice dimension, counted around the lattice (the lattice closes on itself in both dimensions).
All inputs are finite; a program needn't handle non-finite values.
Results may differ from a plain program's by a relative error of at most 0.0003.
Values may be sent and summed in bfloat16 or wider, within the bound.
A program may use at most 128 MiB of HBM per device.

v0:
```python
import math

import jax
import jax.numpy as jnp
import numpy as np
from jax import lax
from jax.experimental import pallas as pl
from jax.experimental.pallas import tpu as pltpu
from jax.sharding import PartitionSpec as P

MESH = pl.DeviceIdType.MESH
STEPS = 32
BLOCK = 384
LINKS = 10
CASES = 32
SITES = 4
TM = 8
ALPHA = 0.5
OWN_STEPS = STEPS // TM
OWN_CASES = CASES // TM
ROWS = OWN_STEPS * OWN_CASES
COLS = STEPS * OWN_CASES


def tables():
    rate = math.log(ALPHA) / STEPS
    root = ALPHA ** (1.0 / STEPS)
    n = np.arange(STEPS)
    k = np.arange(STEPS // 2)
    angle = 2.0 * np.pi / STEPS * ((n[:, None] * k[None, :]) % STEPS)
    real, imag = np.cos(angle), -np.sin(angle)
    alternate = np.where(n % 2 == 0, 1.0, -1.0)
    imag[:, 0] = alternate
    forward = np.concatenate([real, imag], axis=1) * np.exp(n * rate)[:, None]
    back_real, back_imag = 2.0 * np.cos(angle), -2.0 * np.sin(angle)
    back_real[:, 0] = 1.0
    back_imag[:, 0] = alternate
    backward = np.concatenate([back_real, back_imag], axis=1) / STEPS * np.exp(-n * rate)[:, None]
    eye = np.eye(OWN_CASES)
    theta = 2.0 * np.pi * k / STEPS
    shift_re = np.concatenate([1.0 - root * np.cos(theta)] * 2)
    shift_re[STEPS // 2] = 1.0 + root
    shift_im = np.concatenate([root * np.sin(theta), -root * np.sin(theta)])
    shift_im[0] = shift_im[STEPS // 2] = 0.0
    shifts = np.zeros((8, COLS))
    shifts[0] = np.repeat(shift_re, OWN_CASES)
    shifts[1] = np.repeat(shift_im, OWN_CASES)
    as_f32 = lambda a: np.asarray(a, np.float32)
    return as_f32(np.kron(forward, eye)), as_f32(np.kron(backward, eye)), as_f32(shifts)


def kernel(xs, stiff_hbm, seg, conn, mass, diag, fwd, bwd, shifts, out,
           stiff, recv, ext_first, ext_second, source, coef_a, coef_b, result,
           stiff_sem, in_send, in_recv, own_sem, halo_send, halo_recv, out_send, out_recv):
    tm, row, blk = lax.axis_index("tm"), lax.axis_index("row"), lax.axis_index("blk")
    odd = lax.rem(row, 2)
    partner = {"row": row + 1 - 2 * odd}
    outer = {"row": lax.rem(row + 7 + 2 * odd, 8)}
    ahead = {"blk": lax.rem(blk + 1, 4)}
    behind = {"blk": lax.rem(blk + 3, 4)}

    stiff_copy = pltpu.make_async_copy(stiff_hbm, stiff, stiff_sem)
    stiff_copy.start()

    barrier = pltpu.get_barrier_semaphore()
    for step in range(1, TM):
        pl.semaphore_signal(barrier, inc=1, device_id={"tm": lax.rem(tm + step, TM)}, device_id_type=MESH)
    for near in (partner, outer, ahead, behind):
        pl.semaphore_signal(barrier, inc=1, device_id=near, device_id_type=MESH)
    pl.semaphore_wait(barrier, TM - 1 + 4)

    def in_copy(site, step):
        to = lax.rem(tm + step, TM)
        return pltpu.make_async_remote_copy(
            src_ref=xs.at[to, site], dst_ref=recv.at[site, pl.ds(pl.multiple_of(tm * ROWS, ROWS), ROWS)],
            send_sem=in_send.at[site, step], recv_sem=in_recv.at[site, step],
            device_id={"tm": to}, device_id_type=MESH)

    def in_own(site):
        return pltpu.make_async_copy(
            xs.at[tm, site], recv.at[site, pl.ds(pl.multiple_of(tm * ROWS, ROWS), ROWS)], own_sem.at[site])

    def start_in(site, carry):
        in_own(site).start()
        for step in range(1, TM):
            in_copy(site, step).start()
        return carry

    lax.fori_loop(0, SITES, start_in, 0)

    for site in range(SITES):
        a, b = divmod(site, 2)
        mass_t = jnp.broadcast_to(mass[a, b:b + 1, :], (COLS, BLOCK)).T
        diag_t = jnp.broadcast_to(diag[a, b:b + 1, :], (COLS, BLOCK)).T
        diag_re = shifts[0:1, :] * mass_t + diag_t
        diag_im = shifts[1:2, :] * mass_t
        modulus = diag_re * diag_re + diag_im * diag_im
        coef_a[site] = diag_re / modulus
        coef_b[site] = diag_im / modulus

    def apply_inverse(site, update):
        return coef_a[site] * update + coef_b[site] * pltpu.roll(update, COLS // 2, 1)

    exts = (ext_first, ext_second)

    def halo_copy(sweep, kind, site):
        source_at, target_at, to = (
            ((0, 0), (1, 0), partner),
            ((0, 0), (2, 0), outer),
            ((0, 0), (0, 1), ahead),
            ((0, 0), (0, 2), behind),
            ((2, 0), (2, 1), ahead),
            ((2, 0), (2, 2), behind),
            ((0, 1), (1, 1), partner),
            ((0, 2), (1, 2), partner),
        )[kind]
        at = lambda place: exts[sweep].at[place[0] * 3 + place[1], site]
        return pltpu.make_async_remote_copy(
            src_ref=at(source_at), dst_ref=at(target_at),
            send_sem=halo_send.at[sweep, kind, site], recv_sem=halo_recv.at[sweep, kind, site],
            device_id=to, device_id_type=MESH)

    def send_own(sweep, site):
        for kind in (1, 2, 3, 0):
            halo_copy(sweep, kind, site).start()

    def pass_on(sweep):
        def forward(site, carry):
            halo_copy(sweep, 1, site).wait_recv()
            halo_copy(sweep, 4, site).start()
            halo_copy(sweep, 5, site).start()
            halo_copy(sweep, 2, site).wait_recv()
            halo_copy(sweep, 6, site).start()
            halo_copy(sweep, 3, site).wait_recv()
            halo_copy(sweep, 7, site).start()
            return carry

        def finish(site, carry):
            for kind in (0, 4, 5, 6, 7):
                halo_copy(sweep, kind, site).wait_recv()
            return carry

        lax.fori_loop(0, SITES, forward, 0)
        lax.fori_loop(0, SITES, finish, 0)

    def transform(site, carry):
        in_own(site).wait()
        for step in range(1, TM):
            in_copy(site, step).wait_recv()
        spectrum = jnp.dot(recv[site].T, fwd[...], precision=lax.Precision.HIGHEST, preferred_element_type=jnp.float32)
        source[site] = spectrum
        ext_first[0, site] = apply_inverse(site, spectrum).astype(jnp.bfloat16)
        send_own(0, site)
        return carry

    lax.fori_loop(0, SITES, transform, 0)
    pass_on(0)
    stiff_copy.wait()

    def relaxed(sweep, site):
        total = jnp.zeros((BLOCK, COLS), jnp.float32)
        for link in range(LINKS):
            place = site * LINKS + link
            up = lax.rem(conn[place * 2] - 2 * row + 18, 16)
            across = lax.rem(conn[place * 2 + 1] - 2 * blk + 10, 8)
            up_block, across_block = up // 2, across // 2
            row_place = jnp.where(up_block == 1, 0, jnp.where(up_block == 2 - 2 * odd, 1, 2))
            col_place = jnp.where(across_block == 1, 0, jnp.where(across_block == 0, 1, 2))
            named = exts[sweep][row_place * 3 + col_place, lax.rem(up, 2) * 2 + lax.rem(across, 2)]
            product = jnp.dot(stiff[place], named, preferred_element_type=jnp.float32)
            total = total + product * seg[place].astype(jnp.float32)
        return apply_inverse(site, source[site] - total)

    def first_sweep(site, carry):
        ext_second[0, site] = relaxed(0, site).astype(jnp.bfloat16)
        send_own(1, site)
        return carry

    lax.fori_loop(0, SITES, first_sweep, 0)
    pass_on(1)

    def out_copy(site, step):
        to = lax.rem(tm + step, TM)
        return pltpu.make_async_remote_copy(
            src_ref=result.at[site, pl.ds(pl.multiple_of(to * ROWS, ROWS), ROWS)], dst_ref=out.at[tm, site],
            send_sem=out_send.at[site, step], recv_sem=out_recv.at[site, step],
            device_id={"tm": to}, device_id_type=MESH)

    def out_own(site):
        return pltpu.make_async_copy(
            result.at[site, pl.ds(pl.multiple_of(tm * ROWS, ROWS), ROWS)], out.at[tm, site], own_sem.at[site])

    def second_sweep(site, carry):
        signal = lax.dot_general(bwd[...], relaxed(1, site), (((1,), (1,)), ((), ())),
                                 precision=lax.Precision.HIGHEST, preferred_element_type=jnp.float32)
        result[site] = signal
        out_own(site).start()
        for step in range(1, TM):
            out_copy(site, step).start()
        return carry

    lax.fori_loop(0, SITES, second_sweep, 0)

    def drain(site, carry):
        for sweep in range(2):
            for kind in range(8):
                halo_copy(sweep, kind, site).wait_send()
        for step in range(1, TM):
            in_copy(site, step).wait_send()
            out_copy(site, step).wait_send()
            out_copy(site, step).wait_recv()
        out_own(site).wait()
        return carry

    lax.fori_loop(0, SITES, drain, 0)


def shards(right_side, stiffness, segments, connectivity, lumped_mass, stiff_diag):
    fwd, bwd, shifts = tables()
    blocks = right_side.reshape(OWN_STEPS, TM, OWN_CASES, SITES, BLOCK)
    xs = jnp.transpose(blocks, (1, 3, 0, 2, 4)).reshape(TM, SITES, ROWS, BLOCK)
    vmem = pl.BlockSpec(memory_space=pltpu.VMEM)
    smem = pl.BlockSpec(memory_space=pltpu.SMEM)
    anywhere = pl.BlockSpec(memory_space=pl.ANY)
    dma = pltpu.SemaphoreType.DMA
    out = pl.pallas_call(
        kernel,
        out_shape=jax.ShapeDtypeStruct((TM, SITES, ROWS, BLOCK), jnp.float32),
        in_specs=[anywhere, anywhere, smem, smem, vmem, vmem, vmem, vmem, vmem],
        out_specs=vmem,
        scratch_shapes=[
            pltpu.VMEM((SITES * LINKS, BLOCK, BLOCK), jnp.bfloat16),
            pltpu.VMEM((SITES, COLS, BLOCK), jnp.float32),
            pltpu.VMEM((9, SITES, BLOCK, COLS), jnp.bfloat16),
            pltpu.VMEM((9, SITES, BLOCK, COLS), jnp.bfloat16),
            pltpu.VMEM((SITES, BLOCK, COLS), jnp.float32),
            pltpu.VMEM((SITES, BLOCK, COLS), jnp.float32),
            pltpu.VMEM((SITES, BLOCK, COLS), jnp.float32),
            pltpu.VMEM((SITES, COLS, BLOCK), jnp.float32),
            dma,
            dma((SITES, TM)),
            dma((SITES, TM)),
            dma((SITES,)),
            dma((2, 8, SITES)),
            dma((2, 8, SITES)),
            dma((SITES, TM)),
            dma((SITES, TM)),
        ],
        compiler_params=pltpu.CompilerParams(
            collective_id=0, has_side_effects=True, vmem_limit_bytes=48 * 2**20),
    )(xs, stiffness.reshape(SITES * LINKS, BLOCK, BLOCK), segments.reshape(-1), connectivity.reshape(-1),
      lumped_mass, stiff_diag, fwd, bwd, shifts)
    steps = out.reshape(TM, SITES, OWN_STEPS, OWN_CASES, BLOCK)
    return jnp.transpose(steps, (2, 0, 3, 1, 4)).reshape(right_side.shape)


def solution(mesh):
    placed = (
        P("tm", None, "row", "blk", None),
        P("row", "blk", None, None, None),
        P("row", "blk", None),
        P("row", "blk", None, None),
        P("row", "blk", None),
        P("row", "blk", None),
    )
    return jax.shard_map(
        shards,
        mesh=mesh,
        in_specs=placed,
        out_specs=P("tm", None, "row", "blk", None),
        check_vma=False,
    )
```

profile of v0, /device:TPU:8, one launch (start us, length us, event | category | flops | bytes accessed | tf_op | source)
XLA Modules:
  0.0 96.0 jit_solution(5326279904801471374)
XLA Ops:
  0.0 0.8 reshape.24.seg
  0.8 0.8 copy.14
  1.6 0.1 reshape.25.conn
  1.7 1.8 %reshape.21 = f32[4,8,4,4,384]{4,3,2,1,0:T(4,128)S(1)} reshape(f32[4,32,2,2,384]{4,3,2,1,0:T(2,128)} %param.9) | data formatting | bytes 1572864 | tf_op jit(solution)/shard_map/reshape | solution.py:220
  3.5 0.2 copy.17
  3.7 0.3 reshape.22.xs
  4.0 0.0 copy-start
  4.0 0.8 copy-done
  4.8 0.0 copy-start.1
  4.8 0.8 copy-done.1
  5.7 0.0 copy-start.2
  5.7 0.7 copy-done.2
  6.4 0.0 copy-start.3
  6.4 0.7 copy-done.3
  7.0 0.0 copy-start.4
  7.0 0.7 copy-done.4
  7.7 86.2 %shard_map.91 = f32[8,4,16,384]{3,2,1,0:T(8,128)S(1)} custom-call(f32[8,4,16,384]{3,2,1,0:T(8,128)S(1)} %reshape.22.xs, bf16[40,384,384]{2,1,0:T(8,128)(2,1)} %bitcast.7, s32[40]{0:T(128)S(1)} %reshape.24.seg, s32[80]{0:T(128)S(1)} %reshape.25.conn, f32[2,2,384]{2,1,0:T(2,128)S(1)} %copy-done.2, f32[2,2,384]{2,1,0:T(2,128)S(1)} %copy-done.3, ...), custom_call_target="tpu_custom_call" | custom-call | tf_op jit(solution)/shard_map/pallas_call | solution.py:226
  93.9 0.2 reshape.26
  94.2 0.3 copy.15
  94.5 1.5 %reshape.27 = f32[4,32,2,2,384]{4,3,2,1,0:T(2,128)} reshape(f32[4,8,4,4,384]{4,3,2,1,0:T(4,128)S(1)} %copy.15) | data formatting | bytes 1572864 | tf_op jit(solution)/shard_map/reshape | solution.py:254
Async XLA Ops:
  4.0 0.8 copy-start
  4.8 0.8 copy-start.1
  5.7 0.7 copy-start.2
  6.4 0.7 copy-start.3
  7.0 0.7 copy-start.4
where the time goes:
time: 96.3 us; the launch traced here: 96 us
  Pallas kernels  86.2 us (90%)
  local copies, waits for them, and re-layouts  9.72 us (10%)
    pallas_call x1, Pallas kernels, shards(): pl.pallas_call(kernel, out_shape=jax.ShapeDtypeStruct((TM, SITES, ROWS, B...  86.2 us
    unnamed x11, local copies, waits for them, and re-layouts  4.54 us
    reshape x2, local copies, waits for them, and re-layouts, shards(): blocks = right_side.reshape(OWN_STEPS, TM, OWN_CASES, SITES, BLOCK)  2.02 us

commit v1 on v0

v1 whole, which is shorter than its diff:
```python
import math

import jax
import jax.numpy as jnp
import numpy as np
from jax import lax
from jax.experimental import pallas as pl
from jax.experimental.pallas import tpu as pltpu
from jax.sharding import PartitionSpec as P

MESH = pl.DeviceIdType.MESH
STEPS = 32
BLOCK = 384
LINKS = 10
CASES = 32
SIDE = 2
CHUNKS = 2
GROUPS = CHUNKS * SIDE
TM = 8
ALPHA = 0.5
OWN_STEPS = STEPS // TM
OWN_CASES = CASES // TM
PAIR = OWN_CASES // CHUNKS
ROWS = OWN_STEPS * PAIR * SIDE
COLS = STEPS * PAIR * SIDE


def tables():
    rate = math.log(ALPHA) / STEPS
    root = ALPHA ** (1.0 / STEPS)
    n = np.arange(STEPS)
    k = np.arange(STEPS // 2)
    angle = 2.0 * np.pi / STEPS * ((n[:, None] * k[None, :]) % STEPS)
    real, imag = np.cos(angle), -np.sin(angle)
    alternate = np.where(n % 2 == 0, 1.0, -1.0)
    imag[:, 0] = alternate
    forward = np.concatenate([real, imag], axis=1) * np.exp(n * rate)[:, None]
    back_real, back_imag = 2.0 * np.cos(angle), -2.0 * np.sin(angle)
    back_real[:, 0] = 1.0
    back_imag[:, 0] = alternate
    backward = np.concatenate([back_real, back_imag], axis=1) / STEPS * np.exp(-n * rate)[:, None]
    eye = np.eye(PAIR * SIDE)
    theta = 2.0 * np.pi * k / STEPS
    shift_re = np.concatenate([1.0 - root * np.cos(theta)] * 2)
    shift_re[STEPS // 2] = 1.0 + root
    shift_im = np.concatenate([root * np.sin(theta), -root * np.sin(theta)])
    shift_im[0] = shift_im[STEPS // 2] = 0.0
    shifts = np.zeros((8, COLS))
    shifts[0] = np.repeat(shift_re, PAIR * SIDE)
    shifts[1] = np.repeat(shift_im, PAIR * SIDE)
    as_f32 = lambda a: np.asarray(a, np.float32)
    return as_f32(np.kron(forward, eye)), as_f32(np.kron(backward, eye)), as_f32(shifts)


def kernel(right, stiff_hbm, seg, conn, mass_hbm, diag_hbm, fwd_hbm, bwd_hbm, shifts_hbm, out,
           stiff, mass, diag, fwd, bwd, shifts, given, coded, recv, scale_given, scale_recv,
           ext00, ext01, ext10, ext11, source, coef_a, coef_b,
           result, landed, scale_result, scale_landed, final,
           load_sem, in_send, in_recv, own_sem, scale_send, scale_sem, halo_send, halo_recv,
           out_send, out_recv, out_scale_send, out_scale_recv):
    tm, row, blk = lax.axis_index("tm"), lax.axis_index("row"), lax.axis_index("blk")
    odd = lax.rem(row, 2)
    partner = {"row": row + 1 - 2 * odd}
    outer = {"row": lax.rem(row + 7 + 2 * odd, 8)}
    ahead = {"blk": lax.rem(blk + 1, 4)}
    behind = {"blk": lax.rem(blk + 3, 4)}
    exts = ((ext00, ext01), (ext10, ext11))

    loads = [
        pltpu.make_async_copy(source_ref, target_ref, load_sem.at[place])
        for place, (source_ref, target_ref) in enumerate((
            (right, given), (mass_hbm, mass), (diag_hbm, diag), (shifts_hbm, shifts), (fwd_hbm, fwd), (bwd_hbm, bwd), (stiff_hbm, stiff)))
    ]
    for load in loads:
        load.start()

    barrier = pltpu.get_barrier_semaphore()
    for step in range(1, TM):
        pl.semaphore_signal(barrier, inc=1, device_id={"tm": lax.rem(tm + step, TM)}, device_id_type=MESH)
    for near in (partner, outer, ahead, behind):
        pl.semaphore_signal(barrier, inc=1, device_id=near, device_id_type=MESH)

    lane = lax.broadcasted_iota(jnp.int32, (1, COLS), 1)

    def encode(value):
        largest = jnp.maximum(jnp.max(jnp.abs(value), axis=1, keepdims=True), 1e-30)
        whole = jnp.round(value * (32767.0 / largest)).astype(jnp.int32).astype(jnp.int16)
        scales = jnp.broadcast_to(largest * (1.0 / 32767.0), (COLS, COLS)).T
        return whole, scales[0:1, :]

    def own_scales(row_from):
        scales = jnp.zeros((1, COLS), jnp.float32)
        for step in range(TM):
            moved = pltpu.roll(row_from(step), lax.rem((step - tm + TM) * ROWS, COLS), 1)
            scales = jnp.where(lane // ROWS == step, moved, scales)
        return scales

    loads[0].wait()

    def code(group, carry):
        chunk, a = group // SIDE, lax.rem(group, SIDE)
        value = jnp.concatenate([given[:, to, chunk, :, a].reshape(ROWS, BLOCK) for to in range(TM)], axis=0)
        coded[group], scale_given[group] = encode(value)
        return carry

    lax.fori_loop(0, GROUPS, code, 0)
    scale_recv[tm] = scale_given[...]
    pl.semaphore_wait(barrier, TM - 1 + 4)

    def scale_copy(step):
        return pltpu.make_async_remote_copy(
            src_ref=scale_given, dst_ref=scale_recv.at[tm], send_sem=scale_send.at[step], recv_sem=scale_sem.at[step],
            device_id={"tm": lax.rem(tm + step, TM)}, device_id_type=MESH)

    def rows_of(owner):
        return pl.ds(pl.multiple_of(owner * ROWS, ROWS), ROWS)

    def in_copy(group, step):
        to = lax.rem(tm + step, TM)
        return pltpu.make_async_remote_copy(
            src_ref=coded.at[group, rows_of(to)], dst_ref=recv.at[group, rows_of(tm)],
            send_sem=in_send.at[group, step], recv_sem=in_recv.at[group, step],
            device_id={"tm": to}, device_id_type=MESH)

    def in_own(group):
        return pltpu.make_async_copy(coded.at[group, rows_of(tm)], recv.at[group, rows_of(tm)], own_sem.at[group])

    def start_in(group, carry):
        in_own(group).start()
        for step in range(1, TM):
            in_copy(group, step).start()
        return carry

    for step in range(1, TM):
        scale_copy(step).start()
    lax.fori_loop(0, GROUPS, start_in, 0)

    first_block = lax.rem(lane, 2) == 0
    for load in loads[1:4]:
        load.wait()

    def by_column(ref, lattice_row):
        column = lambda b: jnp.broadcast_to(ref[lattice_row, b:b + 1, :], (COLS, BLOCK)).T
        return jnp.where(first_block, column(0), column(1))

    for a in range(SIDE):
        mass_t, diag_t = by_column(mass, a), by_column(diag, a)
        diag_re = shifts[0:1, :] * mass_t + diag_t
        diag_im = shifts[1:2, :] * mass_t
        modulus = diag_re * diag_re + diag_im * diag_im
        coef_a[a] = diag_re / modulus
        coef_b[a] = diag_im / modulus
    for load in loads[4:6]:
        load.wait()

    def apply_inverse(a, update):
        return coef_a[a] * update + coef_b[a] * pltpu.roll(update, COLS // 2, 1)

    def halo_copy(sweep, kind, chunk, a):
        source_at, target_at, to = (
            ((0, 0), (1, 0), partner),
            ((0, 0), (2, 0), outer),
            ((0, 0), (0, 1), ahead),
            ((0, 0), (0, 2), behind),
            ((2, 0), (2, 1), ahead),
            ((2, 0), (2, 2), behind),
            ((0, 1), (1, 1), partner),
            ((0, 2), (1, 2), partner),
        )[kind]
        at = lambda place: exts[sweep][chunk].at[place[0] * 3 + place[1], a]
        group = chunk * SIDE + a
        return pltpu.make_async_remote_copy(
            src_ref=at(source_at), dst_ref=at(target_at),
            send_sem=halo_send.at[sweep, kind, group], recv_sem=halo_recv.at[sweep, kind, group],
            device_id=to, device_id_type=MESH)

    def send_own(sweep, chunk, a):
        for kind in (1, 2, 3, 0):
            halo_copy(sweep, kind, chunk, a).start()

    def over_rows(body):
        def step(a, carry):
            body(a)
            return carry
        lax.fori_loop(0, SIDE, step, 0)

    def pass_across(sweep, chunk):
        def body(a):
            halo_copy(sweep, 1, chunk, a).wait_recv()
            halo_copy(sweep, 4, chunk, a).start()
            halo_copy(sweep, 5, chunk, a).start()
        over_rows(body)

    def pass_partner(sweep, chunk):
        def body(a):
            halo_copy(sweep, 2, chunk, a).wait_recv()
            halo_copy(sweep, 6, chunk, a).start()
            halo_copy(sweep, 3, chunk, a).wait_recv()
            halo_copy(sweep, 7, chunk, a).start()
        over_rows(body)

    def arrive(sweep, chunk):
        def body(a):
            for kind in (0, 4, 5, 6, 7):
                halo_copy(sweep, kind, chunk, a).wait_recv()
        over_rows(body)

    def transform(chunk):
        def body(a):
            group = chunk * SIDE + a
            in_own(group).wait()
            for step in range(1, TM):
                in_copy(group, step).wait_recv()
            steps = recv[group].astype(jnp.int32).astype(jnp.float32).T * own_scales(lambda step: scale_recv[step, group])
            spectrum = jnp.dot(steps, fwd[...],
                               precision=lax.Precision.HIGHEST, preferred_element_type=jnp.float32)
            source[group] = spectrum
            exts[0][chunk][0, a] = apply_inverse(a, spectrum).astype(jnp.bfloat16)
            send_own(0, chunk, a)
        over_rows(body)

    def relaxed(sweep, chunk, a):
        parts = []
        for b in range(SIDE):
            total = jnp.zeros((BLOCK, COLS), jnp.float32)
            for link in range(LINKS):
                up = lax.rem(conn[a, b, 0, link] - 2 * row + 18, 16)
                across = lax.rem(conn[a, b, 1, link] - 2 * blk + 10, 8)
                up_block, across_block = up // 2, across // 2
                row_place = jnp.where(up_block == 1, 0, jnp.where(up_block == 2 - 2 * odd, 1, 2))
                col_place = jnp.where(across_block == 1, 0, jnp.where(across_block == 0, 1, 2))
                named = exts[sweep][chunk][row_place * 3 + col_place, lax.rem(up, 2)]
                product = jnp.dot(stiff[(a * SIDE + b) * LINKS + link], named, preferred_element_type=jnp.float32)
                factor = seg[a, b, link].astype(jnp.float32)
                total = total + product * jnp.where(first_block == (lax.rem(across, 2) == 0), factor, 0.0)
            parts.append(total)
        mine = jnp.where(first_block, parts[0], parts[1])
        other = jnp.where(first_block, parts[1], parts[0])
        other = jnp.where(first_block, pltpu.roll(other, COLS - 1, 1), pltpu.roll(other, 1, 1))
        return apply_inverse(a, source[chunk * SIDE + a] - (mine + other))

    def first_sweep(chunk):
        def body(a):
            exts[1][chunk][0, a] = relaxed(0, chunk, a).astype(jnp.bfloat16)
            send_own(1, chunk, a)
        over_rows(body)

    def out_copy(group, step):
        to = lax.rem(tm + step, TM)
        return pltpu.make_async_remote_copy(
            src_ref=result.at[group, rows_of(to)], dst_ref=landed.at[group, rows_of(tm)],
            send_sem=out_send.at[group, step], recv_sem=out_recv.at[group, step],
            device_id={"tm": to}, device_id_type=MESH)

    def out_scale(group, step):
        return pltpu.make_async_remote_copy(
            src_ref=scale_result.at[group], dst_ref=scale_landed.at[group, tm],
            send_sem=out_scale_send.at[group, step], recv_sem=out_scale_recv.at[group, step],
            device_id={"tm": lax.rem(tm + step, TM)}, device_id_type=MESH)

    def out_own(group):
        return pltpu.make_async_copy(result.at[group, rows_of(tm)], landed.at[group, rows_of(tm)], own_sem.at[group])

    def second_sweep(chunk):
        def body(a):
            group = chunk * SIDE + a
            signal = lax.dot_general(bwd[...], relaxed(1, chunk, a), (((1,), (1,)), ((), ())),
                                     precision=lax.Precision.HIGHEST, preferred_element_type=jnp.float32)
            result[group], scale_result[group] = encode(signal)
            scale_landed[group, tm] = scale_result[group]
            for step in range(1, TM):
                out_scale(group, step).start()
                out_copy(group, step).start()
            out_own(group).start()
        over_rows(body)

    def final_copy(chunk, a):
        return pltpu.make_async_copy(
            final.at[:, :, chunk, :, a], out.at[:, :, chunk, :, a], in_send.at[chunk * SIDE + a, 0])

    def finish(chunk):
        def body(a):
            group = chunk * SIDE + a
            out_own(group).wait()
            for step in range(1, TM):
                out_copy(group, step).wait_recv()
                out_scale(group, step).wait_recv()
            scales = jnp.broadcast_to(own_scales(lambda step: scale_landed[group, step]), (COLS, COLS)).T
            value = landed[group].astype(jnp.int32).astype(jnp.float32) * jnp.concatenate([scales] * (BLOCK // COLS), axis=1)
            for step in range(TM):
                part = value[step * ROWS:(step + 1) * ROWS]
                final[:, step, chunk, :, a] = part.reshape(OWN_STEPS, PAIR, SIDE, BLOCK)
            final_copy(chunk, a).start()
        over_rows(body)

    for step in range(1, TM):
        scale_copy(step).wait_recv()
    transform(0)
    pass_across(0, 0)
    transform(1)
    pass_partner(0, 0)
    pass_across(0, 1)
    arrive(0, 0)
    loads[6].wait()
    first_sweep(0)
    pass_partner(0, 1)
    pass_across(1, 0)
    arrive(0, 1)
    first_sweep(1)
    pass_partner(1, 0)
    pass_across(1, 1)
    arrive(1, 0)
    second_sweep(0)
    pass_partner(1, 1)
    arrive(1, 1)
    second_sweep(1)

    finish(0)
    finish(1)

    def drain(group, carry):
        for step in range(1, TM):
            in_copy(group, step).wait_send()
            out_copy(group, step).wait_send()
            out_scale(group, step).wait_send()
        final_copy(group // SIDE, lax.rem(group, SIDE)).wait()
        return carry

    for step in range(1, TM):
        scale_copy(step).wait_send()
    lax.fori_loop(0, GROUPS, drain, 0)
    for sweep in range(2):
        for chunk in range(CHUNKS):
            over_rows(lambda a: [halo_copy(sweep, kind, chunk, a).wait_send() for kind in range(8)])


def shards(right_side, stiffness, segments, connectivity, lumped_mass, stiff_diag):
    smem = pl.BlockSpec(memory_space=pltpu.SMEM)
    hbm = pl.BlockSpec(memory_space=pltpu.HBM)
    dma = pltpu.SemaphoreType.DMA
    ext = pltpu.VMEM((9, SIDE, BLOCK, COLS), jnp.bfloat16)
    split = (OWN_STEPS, TM, CHUNKS, PAIR, SIDE, SIDE, BLOCK)
    rows = pltpu.VMEM((GROUPS, COLS, BLOCK), jnp.int16)
    result = pl.pallas_call(
        kernel,
        out_shape=jax.ShapeDtypeStruct(split, jnp.float32),
        in_specs=[hbm, hbm, smem, smem, hbm, hbm, hbm, hbm, hbm],
        out_specs=hbm,
        scratch_shapes=[
            pltpu.VMEM((SIDE * SIDE * LINKS, BLOCK, BLOCK), jnp.bfloat16),
            pltpu.VMEM(lumped_mass.shape, jnp.float32),
            pltpu.VMEM(stiff_diag.shape, jnp.float32),
            pltpu.VMEM((COLS, COLS), jnp.float32),
            pltpu.VMEM((COLS, COLS), jnp.float32),
            pltpu.VMEM((8, COLS), jnp.float32),
            pltpu.VMEM(split, jnp.float32),
            rows,
            rows,
            pltpu.VMEM((GROUPS, 1, COLS), jnp.float32),
            pltpu.VMEM((TM, GROUPS, 1, COLS), jnp.float32),
            ext, ext, ext, ext,
            pltpu.VMEM((GROUPS, BLOCK, COLS), jnp.float32),
            pltpu.VMEM((SIDE, BLOCK, COLS), jnp.float32),
            pltpu.VMEM((SIDE, BLOCK, COLS), jnp.float32),
            rows,
            rows,
            pltpu.VMEM((GROUPS, 1, COLS), jnp.float32),
            pltpu.VMEM((GROUPS, TM, 1, COLS), jnp.float32),
            pltpu.VMEM(split, jnp.float32),
            dma((7,)),
            dma((GROUPS, TM)),
            dma((GROUPS, TM)),
            dma((GROUPS,)),
            dma((TM,)),
            dma((TM,)),
            dma((2, 8, GROUPS)),
            dma((2, 8, GROUPS)),
            dma((GROUPS, TM)),
            dma((GROUPS, TM)),
            dma((GROUPS, TM)),
            dma((GROUPS, TM)),
        ],
        compiler_params=pltpu.CompilerParams(
            collective_id=0, has_side_effects=True, vmem_limit_bytes=60 * 2**20),
    )(right_side.reshape(split), stiffness.reshape(SIDE * SIDE * LINKS, BLOCK, BLOCK), segments,
      jnp.transpose(connectivity, (0, 1, 3, 2)), lumped_mass, stiff_diag, *tables())
    return result.reshape(right_side.shape)


def solution(mesh):
    placed = (
        P("tm", None, "row", "blk", None),
        P("row", "blk", None, None, None),
        P("row", "blk", None),
        P("row", "blk", None, None),
        P("row", "blk", None),
        P("row", "blk", None),
    )
    return jax.shard_map(
        shards,
        mesh=mesh,
        in_specs=placed,
        out_specs=P("tm", None, "row", "blk", None),
        check_vma=False,
    )
```

time: 96.3 us -> 76.1 us (0.79)
  the two profiles are of different devices: /device:TPU:8 before, /device:TPU:1 now
where the time goes in v1:
time: 76.1 us; the launch traced here: 76 us
  Pallas kernels  73.7 us (97%)
  local copies, waits for them, and re-layouts  2.28 us (3%)
    pallas_call x1, Pallas kernels, shards(): pl.pallas_call(kernel, out_shape=jax.ShapeDtypeStruct(split, jnp.float32)...  73.7 us
    unnamed x1, local copies, waits for them, and re-layouts  2.28 us

profile of v1, /device:TPU:1, one launch (start us, length us, event | category | flops | bytes accessed | tf_op | source)
XLA Modules:
  0.0 76.0 jit_solution(11494830212573835460)
XLA Ops:
  0.0 73.7 %shard_map.91 = f32[4,8,2,2,2,2,384]{6,5,4,3,2,1,0:T(2,128)} custom-call(f32[4,8,2,2,2,2,384]{6,5,4,3,2,1,0:T(2,128)} %bitcast.6, bf16[40,384,384]{2,1,0:T(8,128)(2,1)} %bitcast.4, s32[2,2,10]{2,1,0:T(2,128)} %seg.1, s32[2,2,2,10]{3,2,1,0:T(2,128)} %bitcast.7, f32[2,2,384]{2,1,0:T(2,128)} %mass_hbm.1, f32[2,2,384]{2,1,0:T(2,128)} %diag_hbm.1, ...), custom_call_target="tpu_custom_call" | custom-call | tf_op jit(solution)/shard_map/pallas_call | solution.py:344
  73.7 2.3 %copy.11 = f32[4,32,2,2,384]{4,3,2,1,0:T(2,128)} copy(f32[4,32,2,2,384]{4,3,2,1,0:T(2,128)} %bitcast.5) | data formatting | bytes 1572864

commit v2 on v1

--- a/solution.py
+++ b/solution.py
@@ -52,12 +52,41 @@
     return as_f32(np.kron(forward, eye)), as_f32(np.kron(backward, eye)), as_f32(shifts)
 
 
-def kernel(right, stiff_hbm, seg, conn, mass_hbm, diag_hbm, fwd_hbm, bwd_hbm, shifts_hbm, out,
-           stiff, mass, diag, fwd, bwd, shifts, given, coded, recv, scale_given, scale_recv,
+def own_scales(tm, row_from):
+    lane = lax.broadcasted_iota(jnp.int32, (1, COLS), 1)
+    scales = jnp.zeros((1, COLS), jnp.float32)
+    for step in range(TM):
+        moved = pltpu.roll(row_from(step), lax.rem((step - tm + TM) * ROWS, COLS), 1)
+        scales = jnp.where(lane // ROWS == step, moved, scales)
+    return scales
+
+
+OTHERS = range(1, TM)
+
+
+def other(tm, step):
+    half, place = tm // 4, lax.rem(tm, 4)
+    return lax.rem(half + (step <= 4), 2) * 4 + lax.rem(place + (step if step <= 4 else step - 4), 4)
+
+
+def copy_kernel(given, out, held, load_sem, store_sem):
+    load = [pltpu.make_async_copy(given.at[step], held.at[step], load_sem.at[step]) for step in range(OWN_STEPS)]
+    store = [pltpu.make_async_copy(held.at[step], out.at[step], store_sem.at[step]) for step in range(OWN_STEPS)]
+    for copy in load:
+        copy.start()
+    for here, there in zip(load, store):
+        here.wait()
+        there.start()
+    for copy in store:
+        copy.wait()
+
+
+def kernel(right, stiff_hbm, seg_hbm, conn_hbm, mass_hbm, diag_hbm, fwd_hbm, bwd_hbm, shifts_hbm, out,
+           stiff, seg, conn, mass, diag, fwd, bwd, shifts, given, coded, recv, scale_given, scale_recv,
            ext00, ext01, ext10, ext11, source, coef_a, coef_b,
-           result, landed, scale_result, scale_landed, final,
-           load_sem, in_send, in_recv, own_sem, scale_send, scale_sem, halo_send, halo_recv,
-           out_send, out_recv, out_scale_send, out_scale_recv):
+           result, scale_result, landed, scale_landed, final,
+           load_sem, in_send, in_recv, own_sem, own_scale_sem, scale_send, scale_sem, halo_send, halo_recv,
+           out_send, out_recv, out_scale_send, out_scale_recv, final_sem):
     tm, row, blk = lax.axis_index("tm"), lax.axis_index("row"), lax.axis_index("blk")
     odd = lax.rem(row, 2)
     partner = {"row": row + 1 - 2 * odd}
@@ -66,19 +95,20 @@
     behind = {"blk": lax.rem(blk + 3, 4)}
     exts = ((ext00, ext01), (ext10, ext11))
 
+    barrier = pltpu.get_barrier_semaphore()
+    for step in OTHERS:
+        pl.semaphore_signal(barrier, inc=1, device_id={"tm": other(tm, step)}, device_id_type=MESH)
+    for near in (partner, outer, ahead, behind):
+        pl.semaphore_signal(barrier, inc=1, device_id=near, device_id_type=MESH)
+
     loads = [
         pltpu.make_async_copy(source_ref, target_ref, load_sem.at[place])
         for place, (source_ref, target_ref) in enumerate((
-            (right, given), (mass_hbm, mass), (diag_hbm, diag), (shifts_hbm, shifts), (fwd_hbm, fwd), (bwd_hbm, bwd), (stiff_hbm, stiff)))
+            (right, given), (mass_hbm, mass), (diag_hbm, diag), (shifts_hbm, shifts), (fwd_hbm, fwd), (bwd_hbm, bwd),
+            (seg_hbm, seg), (conn_hbm, conn), (stiff_hbm, stiff)))
     ]
     for load in loads:
         load.start()
-
-    barrier = pltpu.get_barrier_semaphore()
-    for step in range(1, TM):
-        pl.semaphore_signal(barrier, inc=1, device_id={"tm": lax.rem(tm + step, TM)}, device_id_type=MESH)
-    for near in (partner, outer, ahead, behind):
-        pl.semaphore_signal(barrier, inc=1, device_id=near, device_id_type=MESH)
 
     lane = lax.broadcasted_iota(jnp.int32, (1, COLS), 1)
 
@@ -88,13 +118,6 @@
         scales = jnp.broadcast_to(largest * (1.0 / 32767.0), (COLS, COLS)).T
         return whole, scales[0:1, :]
 
-    def own_scales(row_from):
-        scales = jnp.zeros((1, COLS), jnp.float32)
-        for step in range(TM):
-            moved = pltpu.roll(row_from(step), lax.rem((step - tm + TM) * ROWS, COLS), 1)
-            scales = jnp.where(lane // ROWS == step, moved, scales)
-        return scales
-
     loads[0].wait()
 
     def code(group, carry):
@@ -110,13 +133,13 @@
     def scale_copy(step):
         return pltpu.make_async_remote_copy(
             src_ref=scale_given, dst_ref=scale_recv.at[tm], send_sem=scale_send.at[step], recv_sem=scale_sem.at[step],
-            device_id={"tm": lax.rem(tm + step, TM)}, device_id_type=MESH)
+            device_id={"tm": other(tm, step)}, device_id_type=MESH)
 
     def rows_of(owner):
         return pl.ds(pl.multiple_of(owner * ROWS, ROWS), ROWS)
 
     def in_copy(group, step):
-        to = lax.rem(tm + step, TM)
+        to = other(tm, step)
         return pltpu.make_async_remote_copy(
             src_ref=coded.at[group, rows_of(to)], dst_ref=recv.at[group, rows_of(tm)],
             send_sem=in_send.at[group, step], recv_sem=in_recv.at[group, step],
@@ -127,11 +150,11 @@
 
     def start_in(group, carry):
         in_own(group).start()
-        for step in range(1, TM):
+        for step in OTHERS:
             in_copy(group, step).start()
         return carry
 
-    for step in range(1, TM):
+    for step in OTHERS:
         scale_copy(step).start()
     lax.fori_loop(0, GROUPS, start_in, 0)
 
@@ -209,9 +232,9 @@
         def body(a):
             group = chunk * SIDE + a
             in_own(group).wait()
-            for step in range(1, TM):
+            for step in OTHERS:
                 in_copy(group, step).wait_recv()
-            steps = recv[group].astype(jnp.int32).astype(jnp.float32).T * own_scales(lambda step: scale_recv[step, group])
+            steps = recv[group].astype(jnp.int32).astype(jnp.float32).T * own_scales(tm, lambda step: scale_recv[step, group])
             spectrum = jnp.dot(steps, fwd[...],
                                precision=lax.Precision.HIGHEST, preferred_element_type=jnp.float32)
             source[group] = spectrum
@@ -246,7 +269,7 @@
         over_rows(body)
 
     def out_copy(group, step):
-        to = lax.rem(tm + step, TM)
+        to = other(tm, step)
         return pltpu.make_async_remote_copy(
             src_ref=result.at[group, rows_of(to)], dst_ref=landed.at[group, rows_of(tm)],
             send_sem=out_send.at[group, step], recv_sem=out_recv.at[group, step],
@@ -256,10 +279,13 @@
         return pltpu.make_async_remote_copy(
             src_ref=scale_result.at[group], dst_ref=scale_landed.at[group, tm],
             send_sem=out_scale_send.at[group, step], recv_sem=out_scale_recv.at[group, step],
-            device_id={"tm": lax.rem(tm + step, TM)}, device_id_type=MESH)
+            device_id={"tm": other(tm, step)}, device_id_type=MESH)
 
     def out_own(group):
         return pltpu.make_async_copy(result.at[group, rows_of(tm)], landed.at[group, rows_of(tm)], own_sem.at[group])
+
+    def own_scale(group):
+        return pltpu.make_async_copy(scale_result.at[group], scale_landed.at[group, tm], own_scale_sem.at[group])
 
     def second_sweep(chunk):
         def body(a):
@@ -267,8 +293,8 @@
             signal = lax.dot_general(bwd[...], relaxed(1, chunk, a), (((1,), (1,)), ((), ())),
                                      precision=lax.Precision.HIGHEST, preferred_element_type=jnp.float32)
             result[group], scale_result[group] = encode(signal)
-            scale_landed[group, tm] = scale_result[group]
-            for step in range(1, TM):
+            own_scale(group).start()
+            for step in OTHERS:
                 out_scale(group, step).start()
                 out_copy(group, step).start()
             out_own(group).start()
@@ -276,32 +302,36 @@
 
     def final_copy(chunk, a):
         return pltpu.make_async_copy(
-            final.at[:, :, chunk, :, a], out.at[:, :, chunk, :, a], in_send.at[chunk * SIDE + a, 0])
+            final.at[:, :, chunk, :, a], out.at[:, :, chunk, :, a], final_sem.at[chunk * SIDE + a])
 
     def finish(chunk):
         def body(a):
             group = chunk * SIDE + a
             out_own(group).wait()
-            for step in range(1, TM):
+            own_scale(group).wait()
+            for step in OTHERS:
                 out_copy(group, step).wait_recv()
                 out_scale(group, step).wait_recv()
-            scales = jnp.broadcast_to(own_scales(lambda step: scale_landed[group, step]), (COLS, COLS)).T
-            value = landed[group].astype(jnp.int32).astype(jnp.float32) * jnp.concatenate([scales] * (BLOCK // COLS), axis=1)
+            scales = own_scales(tm, lambda step: scale_landed[group, step])
+            scales = jnp.broadcast_to(scales, (COLS, COLS)).T
+            value = landed[group].astype(jnp.int32).astype(jnp.float32) * jnp.concatenate(
+                [scales] * (BLOCK // COLS), axis=1)
             for step in range(TM):
                 part = value[step * ROWS:(step + 1) * ROWS]
                 final[:, step, chunk, :, a] = part.reshape(OWN_STEPS, PAIR, SIDE, BLOCK)
             final_copy(chunk, a).start()
         over_rows(body)
 
-    for step in range(1, TM):
+    for step in OTHERS:
         scale_copy(step).wait_recv()
     transform(0)
+    transform(1)
     pass_across(0, 0)
-    transform(1)
     pass_partner(0, 0)
     pass_across(0, 1)
     arrive(0, 0)
-    loads[6].wait()
+    for load in loads[6:]:
+        load.wait()
     first_sweep(0)
     pass_partner(0, 1)
     pass_across(1, 0)
@@ -314,19 +344,18 @@
     pass_partner(1, 1)
     arrive(1, 1)
     second_sweep(1)
-
     finish(0)
     finish(1)
 
     def drain(group, carry):
-        for step in range(1, TM):
+        for step in OTHERS:
             in_copy(group, step).wait_send()
             out_copy(group, step).wait_send()
             out_scale(group, step).wait_send()
         final_copy(group // SIDE, lax.rem(group, SIDE)).wait()
         return carry
 
-    for step in range(1, TM):
+    for step in OTHERS:
         scale_copy(step).wait_send()
     lax.fori_loop(0, GROUPS, drain, 0)
     for sweep in range(2):
@@ -335,19 +364,22 @@
 
 
 def shards(right_side, stiffness, segments, connectivity, lumped_mass, stiff_diag):
-    smem = pl.BlockSpec(memory_space=pltpu.SMEM)
     hbm = pl.BlockSpec(memory_space=pltpu.HBM)
     dma = pltpu.SemaphoreType.DMA
+    split = (OWN_STEPS, TM, CHUNKS, PAIR, SIDE, SIDE, BLOCK)
+    links = jnp.transpose(connectivity, (0, 1, 3, 2))
     ext = pltpu.VMEM((9, SIDE, BLOCK, COLS), jnp.bfloat16)
-    split = (OWN_STEPS, TM, CHUNKS, PAIR, SIDE, SIDE, BLOCK)
     rows = pltpu.VMEM((GROUPS, COLS, BLOCK), jnp.int16)
-    result = pl.pallas_call(
+    between = dma((GROUPS, TM))
+    decoded = pl.pallas_call(
         kernel,
         out_shape=jax.ShapeDtypeStruct(split, jnp.float32),
-        in_specs=[hbm, hbm, smem, smem, hbm, hbm, hbm, hbm, hbm],
+        in_specs=[hbm] * 9,
         out_specs=hbm,
         scratch_shapes=[
             pltpu.VMEM((SIDE * SIDE * LINKS, BLOCK, BLOCK), jnp.bfloat16),
+            pltpu.SMEM(segments.shape, jnp.int32),
+            pltpu.SMEM(links.shape, jnp.int32),
             pltpu.VMEM(lumped_mass.shape, jnp.float32),
             pltpu.VMEM(stiff_diag.shape, jnp.float32),
             pltpu.VMEM((COLS, COLS), jnp.float32),
@@ -363,27 +395,37 @@
             pltpu.VMEM((SIDE, BLOCK, COLS), jnp.float32),
             pltpu.VMEM((SIDE, BLOCK, COLS), jnp.float32),
             rows,
+            pltpu.VMEM((GROUPS, 1, COLS), jnp.float32),
             rows,
-            pltpu.VMEM((GROUPS, 1, COLS), jnp.float32),
             pltpu.VMEM((GROUPS, TM, 1, COLS), jnp.float32),
             pltpu.VMEM(split, jnp.float32),
-            dma((7,)),
-            dma((GROUPS, TM)),
-            dma((GROUPS, TM)),
+            dma((9,)),
+            between,
+            between,
+            dma((GROUPS,)),
             dma((GROUPS,)),
             dma((TM,)),
             dma((TM,)),
             dma((2, 8, GROUPS)),
             dma((2, 8, GROUPS)),
-            dma((GROUPS, TM)),
-            dma((GROUPS, TM)),
-            dma((GROUPS, TM)),
-            dma((GROUPS, TM)),
+            between,
+            between,
+            between,
+            between,
+            dma((GROUPS,)),
         ],
         compiler_params=pltpu.CompilerParams(
             collective_id=0, has_side_effects=True, vmem_limit_bytes=60 * 2**20),
-    )(right_side.reshape(split), stiffness.reshape(SIDE * SIDE * LINKS, BLOCK, BLOCK), segments,
-      jnp.transpose(connectivity, (0, 1, 3, 2)), lumped_mass, stiff_diag, *tables())
+    )(right_side.reshape(split), stiffness.reshape(SIDE * SIDE * LINKS, BLOCK, BLOCK), segments, links,
+      lumped_mass, stiff_diag, *tables())
+    result = pl.pallas_call(
+        copy_kernel,
+        out_shape=jax.ShapeDtypeStruct(split, jnp.float32),
+        in_specs=[hbm],
+        out_specs=hbm,
+        scratch_shapes=[pltpu.VMEM(split, jnp.float32), dma((OWN_STEPS,)), dma((OWN_STEPS,))],
+        compiler_params=pltpu.CompilerParams(vmem_limit_bytes=60 * 2**20),
+    )(decoded)
     return result.reshape(right_side.shape)
 
 

time: 76.1 us -> 73.7 us (0.968)
  local copies, waits for them, and re-layouts: 2.28 us -> 0 us
    unnamed x1 -> x0, local copies, waits for them, and re-layouts: 2.28 us -> none
    pallas_call x1, Pallas kernels: 73.7 us -> 71.6 us  [shards(): pl.pallas_call(kernel, out_shape=jax.ShapeDtypeStruct(split, jnp.float32)...]
    pallas_call x0 -> x1, Pallas kernels: none -> 1.96 us  [shards(): pl.pallas_call(copy_kernel, out_shape=jax.ShapeDtypeStruct(split, jnp.flo...]
where the time goes in v2:
time: 73.7 us; the launch traced here: 73.6 us
  Pallas kernels  73.6 us (100%)
    pallas_call x1, Pallas kernels, shards(): pl.pallas_call(kernel, out_shape=jax.ShapeDtypeStruct(split, jnp.float32)...  71.6 us
    pallas_call x1, Pallas kernels, shards(): pl.pallas_call(copy_kernel, out_shape=jax.ShapeDtypeStruct(split, jnp.flo...  1.96 us

profile of v2, /device:TPU:1, one launch (start us, length us, event | category | flops | bytes accessed | tf_op | source)
XLA Modules:
  0.0 73.6 jit_solution(13614640144838464846)
XLA Ops:
  0.0 71.6 %shard_map.91.given = f32[4,8,2,2,2,2,384]{6,5,4,3,2,1,0:T(2,128)} custom-call(f32[4,8,2,2,2,2,384]{6,5,4,3,2,1,0:T(2,128)} %bitcast.5, bf16[40,384,384]{2,1,0:T(8,128)(2,1)} %bitcast.4, s32[2,2,10]{2,1,0:T(2,128)} %seg_hbm.1, s32[2,2,2,10]{3,2,1,0:T(2,128)} %bitcast.6, f32[2,2,384]{2,1,0:T(2,128)} %mass_hbm.1, f32[2,2,384]{2,1,0:T(2,128)} %diag_hbm.1, ...), custom_call_target="tpu_custom_call" | custom-call | tf_op jit(solution)/shard_map/pallas_call | solution.py:374
  71.6 2.0 %shard_map.92 = f32[4,8,2,2,2,2,384]{6,5,4,3,2,1,0:T(2,128)} custom-call(f32[4,8,2,2,2,2,384]{6,5,4,3,2,1,0:T(2,128)} %shard_map.91.given), custom_call_target="tpu_custom_call" | custom-call | tf_op jit(solution)/shard_map/pallas_call | solution.py:421

commit v3 on v2

--- a/solution.py
+++ b/solution.py
@@ -69,24 +69,12 @@
     return lax.rem(half + (step <= 4), 2) * 4 + lax.rem(place + (step if step <= 4 else step - 4), 4)
 
 
-def copy_kernel(given, out, held, load_sem, store_sem):
-    load = [pltpu.make_async_copy(given.at[step], held.at[step], load_sem.at[step]) for step in range(OWN_STEPS)]
-    store = [pltpu.make_async_copy(held.at[step], out.at[step], store_sem.at[step]) for step in range(OWN_STEPS)]
-    for copy in load:
-        copy.start()
-    for here, there in zip(load, store):
-        here.wait()
-        there.start()
-    for copy in store:
-        copy.wait()
-
-
 def kernel(right, stiff_hbm, seg_hbm, conn_hbm, mass_hbm, diag_hbm, fwd_hbm, bwd_hbm, shifts_hbm, out,
            stiff, seg, conn, mass, diag, fwd, bwd, shifts, given, coded, recv, scale_given, scale_recv,
            ext00, ext01, ext10, ext11, source, coef_a, coef_b,
-           result, scale_result, landed, scale_landed, final,
+           result, scale_result, landed, scale_landed,
            load_sem, in_send, in_recv, own_sem, own_scale_sem, scale_send, scale_sem, halo_send, halo_recv,
-           out_send, out_recv, out_scale_send, out_scale_recv, final_sem):
+           out_send, out_recv, out_scale_send, out_scale_recv):
     tm, row, blk = lax.axis_index("tm"), lax.axis_index("row"), lax.axis_index("blk")
     odd = lax.rem(row, 2)
     partner = {"row": row + 1 - 2 * odd}
@@ -300,10 +288,6 @@
             out_own(group).start()
         over_rows(body)
 
-    def final_copy(chunk, a):
-        return pltpu.make_async_copy(
-            final.at[:, :, chunk, :, a], out.at[:, :, chunk, :, a], final_sem.at[chunk * SIDE + a])
-
     def finish(chunk):
         def body(a):
             group = chunk * SIDE + a
@@ -318,12 +302,30 @@
                 [scales] * (BLOCK // COLS), axis=1)
             for step in range(TM):
                 part = value[step * ROWS:(step + 1) * ROWS]
-                final[:, step, chunk, :, a] = part.reshape(OWN_STEPS, PAIR, SIDE, BLOCK)
-            final_copy(chunk, a).start()
+                out[:, step, chunk, :, a] = part.reshape(OWN_STEPS, PAIR, SIDE, BLOCK)
         over_rows(body)
 
     for step in OTHERS:
         scale_copy(step).wait_recv()
+    def sent_in():
+        def body(group, carry):
+            for step in OTHERS:
+                in_copy(group, step).wait_send()
+            return carry
+        for step in OTHERS:
+            scale_copy(step).wait_send()
+        lax.fori_loop(0, GROUPS, body, 0)
+
+    def sent_halo(sweep, chunk):
+        over_rows(lambda a: [halo_copy(sweep, kind, chunk, a).wait_send() for kind in range(8)])
+
+    def sent_out(chunk):
+        def body(a):
+            for step in OTHERS:
+                out_copy(chunk * SIDE + a, step).wait_send()
+                out_scale(chunk * SIDE + a, step).wait_send()
+        over_rows(body)
+
     transform(0)
     transform(1)
     pass_across(0, 0)
@@ -338,29 +340,21 @@
     arrive(0, 1)
     first_sweep(1)
     pass_partner(1, 0)
+    sent_in()
+    sent_halo(0, 0)
     pass_across(1, 1)
+    sent_halo(0, 1)
     arrive(1, 0)
     second_sweep(0)
     pass_partner(1, 1)
+    sent_halo(1, 0)
     arrive(1, 1)
     second_sweep(1)
+    sent_halo(1, 1)
     finish(0)
+    sent_out(0)
     finish(1)
-
-    def drain(group, carry):
-        for step in OTHERS:
-            in_copy(group, step).wait_send()
-            out_copy(group, step).wait_send()
-            out_scale(group, step).wait_send()
-        final_copy(group // SIDE, lax.rem(group, SIDE)).wait()
-        return carry
-
-    for step in OTHERS:
-        scale_copy(step).wait_send()
-    lax.fori_loop(0, GROUPS, drain, 0)
-    for sweep in range(2):
-        for chunk in range(CHUNKS):
-            over_rows(lambda a: [halo_copy(sweep, kind, chunk, a).wait_send() for kind in range(8)])
+    sent_out(1)
 
 
 def shards(right_side, stiffness, segments, connectivity, lumped_mass, stiff_diag):
@@ -373,9 +367,9 @@
     between = dma((GROUPS, TM))
     decoded = pl.pallas_call(
         kernel,
-        out_shape=jax.ShapeDtypeStruct(split, jnp.float32),
+        out_shape=pltpu.VMEM(split, jnp.float32),
         in_specs=[hbm] * 9,
-        out_specs=hbm,
+        out_specs=pl.BlockSpec(memory_space=pltpu.VMEM),
         scratch_shapes=[
             pltpu.VMEM((SIDE * SIDE * LINKS, BLOCK, BLOCK), jnp.bfloat16),
             pltpu.SMEM(segments.shape, jnp.int32),
@@ -398,7 +392,6 @@
             pltpu.VMEM((GROUPS, 1, COLS), jnp.float32),
             rows,
             pltpu.VMEM((GROUPS, TM, 1, COLS), jnp.float32),
-            pltpu.VMEM(split, jnp.float32),
             dma((9,)),
             between,
             between,
@@ -412,21 +405,12 @@
             between,
             between,
             between,
-            dma((GROUPS,)),
         ],
         compiler_params=pltpu.CompilerParams(
-            collective_id=0, has_side_effects=True, vmem_limit_bytes=60 * 2**20),
+            collective_id=0, has_side_effects=True, vmem_limit_bytes=56 * 2**20),
     )(right_side.reshape(split), stiffness.reshape(SIDE * SIDE * LINKS, BLOCK, BLOCK), segments, links,
       lumped_mass, stiff_diag, *tables())
-    result = pl.pallas_call(
-        copy_kernel,
-        out_shape=jax.ShapeDtypeStruct(split, jnp.float32),
-        in_specs=[hbm],
-        out_specs=hbm,
-        scratch_shapes=[pltpu.VMEM(split, jnp.float32), dma((OWN_STEPS,)), dma((OWN_STEPS,))],
-        compiler_params=pltpu.CompilerParams(vmem_limit_bytes=60 * 2**20),
-    )(decoded)
-    return result.reshape(right_side.shape)
+    return decoded.reshape(right_side.shape)
 
 
 def solution(mesh):

time: 73.7 us -> 71.8 us (0.974)
  Pallas kernels: 73.6 us -> 70.8 us
  local copies, waits for them, and re-layouts: 0 us -> 0.88 us
    pallas_call x2 -> x1, Pallas kernels: 73.6 us -> 70.8 us  [shards(): pl.pallas_call(kernel, out_shape=pltpu.VMEM(split, jnp.float32), in_specs...]
    unnamed x0 -> x1, local copies, waits for them, and re-layouts: none -> 0.88 us
where the time goes in v3:
time: 71.8 us; the launch traced here: 71.7 us
  Pallas kernels  70.8 us (99%)
  local copies, waits for them, and re-layouts  0.88 us (1%)
    pallas_call x1, Pallas kernels, shards(): pl.pallas_call(kernel, out_shape=pltpu.VMEM(split, jnp.float32), in_specs...  70.8 us

profile of v3, /device:TPU:1, one launch (start us, length us, event | category | flops | bytes accessed | tf_op | source)
XLA Modules:
  0.0 71.7 jit_solution(15349993138738588049)
XLA Ops:
  0.0 70.8 %shard_map.91 = f32[4,8,2,2,2,2,384]{6,5,4,3,2,1,0:T(2,128)S(1)} custom-call(f32[4,8,2,2,2,2,384]{6,5,4,3,2,1,0:T(2,128)} %bitcast.6, bf16[40,384,384]{2,1,0:T(8,128)(2,1)} %bitcast.5, s32[2,2,10]{2,1,0:T(2,128)} %seg_hbm.1, s32[2,2,2,10]{3,2,1,0:T(2,128)} %bitcast.7, f32[2,2,384]{2,1,0:T(2,128)} %mass_hbm.1, f32[2,2,384]{2,1,0:T(2,128)} %diag_hbm.1, ...), custom_call_target="tpu_custom_call" | custom-call | tf_op jit(solution)/shard_map/pallas_call | solution.py:368
  70.9 0.9 %copy.11 = f32[4,32,2,2,384]{4,3,2,1,0:T(2,128)} copy(f32[4,32,2,2,384]{4,3,2,1,0:T(2,128)S(1)} %bitcast.4) | data formatting | bytes 1572864
